TPU v7x, 32 devices: a whole 2x2x4 slice. The times are simulated.
32 devices in a mesh: groups: 2 (over y), tm: 4 (over z), pair: 2 (over x), head: 2 (over core).
Axes of the slice: x: 2, y: 2, z: 4, core: 2. Of those that a mesh axis runs over, the one named last changes fastest.
Arguments:
- gdn_query: bfloat16 [4, 512, 8, 128], P(('groups', 'pair'), 'tm', 'head'), parts along dimension 0, may hold values from -14 to 14
- gdn_key: bfloat16 [4, 512, 8, 128], P(('groups', 'pair'), 'tm', 'head'), parts along dimension 0, may hold values from -12 to 12
- gdn_value: bfloat16 [4, 512, 8, 128], P(('groups', 'pair'), 'tm', 'head'), parts along dimension 0, may hold values from -0.59765625 to 0.59765625
- log_decay: float32 [4, 8, 512], P(('groups', 'pair'), 'head', 'tm'), parts along dimension 0, may hold values from -0.8 to 0
- write_rate: float32 [4, 8, 512], P(('groups', 'pair'), 'head', 'tm'), parts along dimension 0, may hold values from 0.025 to 0.05
- init_state: float32 [4, 8, 128, 128], P(('groups', 'pair'), 'head'), parts along dimension 0, may hold values from -0.5 to 0.5
- attn_query: bfloat16 [4, 512, 8, 128], P(('groups', 'pair'), 'tm', 'head'), parts along dimension 0, may hold values from -6 to 6
- attn_key: bfloat16 [4, 512, 2, 128], P(('groups', 'pair'), 'tm', 'head'), parts along dimension 0, may hold values from -6 to 6
- attn_value: bfloat16 [4, 512, 2, 128], P(('groups', 'pair'), 'tm', 'head'), parts along dimension 0, may hold values from -6 to 6
- readout: bfloat16 [4, 512, 8, 128], P(('groups', 'pair'), 'tm', 'head'), parts along dimension 0, may hold values from -0.1875 to 0.1875
- speaker_mask: int32 [4, 512], P(('groups', 'pair'), 'tm'), parts along dimension 0, may hold values 0 or 1
- pair_slot: int32 [4], P(('groups', 'pair')), parts along dimension 0, may hold values from 0 to 1, each once
- ref_margin: float32 [2], P('groups'), parts along dimension 0, may hold values from -4 to 4
Outputs:
- dpo_loss: float32 [2], P('groups'), parts along dimension 0
- grad_gdn_query: bfloat16 [4, 512, 8, 128], P(('groups', 'pair'), 'tm', 'head'), parts along dimension 0
- grad_gdn_key: bfloat16 [4, 512, 8, 128], P(('groups', 'pair'), 'tm', 'head'), parts along dimension 0
- grad_gdn_value: bfloat16 [4, 512, 8, 128], P(('groups', 'pair'), 'tm', 'head'), parts along dimension 0
- grad_log_decay: float32 [4, 8, 512], P(('groups', 'pair'), 'head', 'tm'), parts along dimension 0
- grad_write_rate: float32 [4, 8, 512], P(('groups', 'pair'), 'head', 'tm'), parts along dimension 0
- grad_attn_query: bfloat16 [4, 512, 8, 128], P(('groups', 'pair'), 'tm', 'head'), parts along dimension 0
- grad_attn_key: bfloat16 [4, 512, 2, 128], P(('groups', 'pair'), 'tm', 'head'), parts along dimension 0
- grad_attn_value: bfloat16 [4, 512, 2, 128], P(('groups', 'pair'), 'tm', 'head'), parts along dimension 0
There are 2 independent parts, one for each index of `groups`. A program takes and returns all parts, laid end to end along the dimension named above; each array names one. Nothing has to cross between parts.
Inputs may be any that keep to these rules, and one draw needn't show every extreme that they name: `pair_slot`: a permutation of 0 to 1; slot // 2 names the pair, an even slot the chosen rollout.
All inputs are finite; a program needn't handle non-finite values. No bound on the sum of `speaker_mask` on one device may be relied on, other than what follows from the above.
Results may differ from a plain program's by a relative error of at most 0.011.
Values may be sent and summed in bfloat16 or wider, within the bound.
A program may use at most 128 MiB of HBM per device.

v0:
```python
import functools

import jax
import jax.numpy as jnp
from jax import lax
from jax.experimental import pallas as pl
from jax.experimental.pallas import tpu as pltpu
from jax.sharding import PartitionSpec as P

WIN = 512
EPSILON = 1e-06
F32 = jnp.float32
BF16 = jnp.bfloat16
NN = (((1,), (0,)), ((), ()))
NT = (((1,), (1,)), ((), ()))
TN = (((0,), (0,)), ((), ()))


def exact(a, b, dims):
    return lax.dot_general(
        a, b, dims, precision=lax.Precision.HIGHEST, preferred_element_type=F32
    )


def quick(a, b, dims):
    return lax.dot_general(
        a.astype(BF16), b.astype(BF16), dims, preferred_element_type=F32
    )


def parts(a):
    high = a.astype(BF16)
    return high, (a - high.astype(F32)).astype(BF16)


def triple(a, b, dims):
    a_high, a_low = parts(a)
    b_high, b_low = parts(b)
    dot = functools.partial(lax.dot_general, dimension_numbers=dims, preferred_element_type=F32)
    return dot(a_high, b_high) + (dot(a_high, b_low) + dot(a_low, b_high))


INVERT = exact
PREP = exact
RELAY = exact
BACK = exact


def unit_lower_inverse(strict, eye):
    power = [-s for s in strict]
    result = [eye + p for p in power]
    span = 2
    while span < eye.shape[0]:
        power = [INVERT(p, p, NN) for p in power]
        result = [r + INVERT(r, p, NN) for r, p in zip(result, power)]
        span *= 2
    return result


def kernel(
    sizes,
    q_ref,
    k_ref,
    v_ref,
    g_ref,
    b_ref,
    s0_ref,
    aq_ref,
    ak_ref,
    av_ref,
    ro_ref,
    mask_ref,
    slot_ref,
    margin_ref,
    loss_ref,
    dq_ref,
    dk_ref,
    dv_ref,
    dg_ref,
    db_ref,
    daq_ref,
    dak_ref,
    dav_ref,
    window,
    back_send,
    back_recv,
    state_send,
    state_recv,
    grad_send,
    grad_recv,
    score_send,
    score_recv,
    kn_s,
    qn_s,
    map_s,
    shift_s,
    qt_s,
    y0_s,
    p_s,
    l_s,
    m_s,
    a_s,
    w_s,
    u_s,
    z_s,
    col_s,
    state_s,
    next_s,
    local_s,
    g_s,
    b0_s,
    delta_s,
    dq_s,
    aq_grad_s,
    own_s,
    row_s,
    win_send_sem,
    win_recv_sem,
    back_send_sem,
    back_recv_sem,
    state_send_sem,
    state_recv_sem,
    grad_send_sem,
    grad_recv_sem,
    score_send_sem,
    score_recv_sem,
):
    n, pairs, halves = sizes
    group = n * pairs * halves
    pos = lax.axis_index("tm")
    me = (pos * pairs + lax.axis_index("pair")) * halves + lax.axis_index("head")
    frames, heads, width = q_ref.shape[1:]
    blocks = window.shape[0]
    total_frames = frames * n

    def place(index):
        return {
            "tm": index // (pairs * halves),
            "pair": (index // halves) % pairs,
            "head": index % halves,
        }

    barrier = pltpu.get_barrier_semaphore()

    def greet(j, c):
        pl.semaphore_signal(
            barrier,
            inc=1,
            device_id=place(lax.rem(me + j, group)),
            device_id_type=pl.DeviceIdType.MESH,
        )
        return c

    lax.fori_loop(1, group, greet, 0)

    def window_copy(d):
        return pltpu.make_async_remote_copy(
            src_ref=window.at[0],
            dst_ref=window.at[d],
            send_sem=win_send_sem.at[d],
            recv_sem=win_recv_sem.at[d],
            device_id={"tm": pos + d},
            device_id_type=pl.DeviceIdType.MESH,
        )

    def back_copy(d):
        return pltpu.make_async_remote_copy(
            src_ref=back_send.at[d - 1],
            dst_ref=back_recv.at[d - 1],
            send_sem=back_send_sem.at[d],
            recv_sem=back_recv_sem.at[d],
            device_id={"tm": pos - d},
            device_id_type=pl.DeviceIdType.MESH,
        )

    def state_copy(h):
        return pltpu.make_async_remote_copy(
            src_ref=state_send.at[h],
            dst_ref=state_recv.at[h],
            send_sem=state_send_sem.at[h],
            recv_sem=state_recv_sem.at[h],
            device_id={"tm": pos + 1},
            device_id_type=pl.DeviceIdType.MESH,
        )

    def grad_copy(h):
        return pltpu.make_async_remote_copy(
            src_ref=grad_send.at[h],
            dst_ref=grad_recv.at[h],
            send_sem=grad_send_sem.at[h],
            recv_sem=grad_recv_sem.at[h],
            device_id={"tm": pos - 1},
            device_id_type=pl.DeviceIdType.MESH,
        )

    def score_copy(source, target):
        return pltpu.make_async_remote_copy(
            src_ref=score_send,
            dst_ref=score_recv.at[source],
            send_sem=score_send_sem.at[target],
            recv_sem=score_recv_sem.at[source],
            device_id=place(target),
            device_id_type=pl.DeviceIdType.MESH,
        )

    window[0, 0] = ak_ref[0, :, 0, :]
    window[0, 1] = av_ref[0, :, 0, :]
    pl.semaphore_wait(barrier, group - 1)
    for d in range(1, blocks):

        @pl.when(pos + d < n)
        def _():
            window_copy(d).start()

        @pl.when(pos < d)
        def _():
            window[d] = jnp.zeros_like(window[d])

    rows = lax.broadcasted_iota(jnp.int32, (frames, frames), 0)
    cols = lax.broadcasted_iota(jnp.int32, (frames, frames), 1)
    lower = rows >= cols
    strict = rows > cols
    tri = jnp.where(lower, 1.0, 0.0).astype(F32)
    eye = jnp.where(rows == cols, 1.0, 0.0).astype(F32)

    gates = jnp.concatenate([g_ref[0], b_ref[0]], axis=0)
    sum_rows = exact(gates, tri, NT)
    sum_cols = exact(tri, gates, NT)
    gate_cols = exact(eye, gates, NT)
    q_all = q_ref[0].astype(F32)
    k_all = k_ref[0].astype(F32)
    v_all = v_ref[0].astype(F32)
    strict_parts = []
    for h in range(heads):
        kh = k_all[:, h, :]
        qh = q_all[:, h, :]
        rk = lax.rsqrt(jnp.sum(kh * kh, axis=-1, keepdims=True) + EPSILON)
        rq = lax.rsqrt(jnp.sum(qh * qh, axis=-1, keepdims=True) + EPSILON)
        kn = kh * rk
        qn = qh * rq
        kn_s[h] = kn
        qn_s[h] = qn
        col_s[h, :, 0:1] = rk
        col_s[h, :, 1:2] = rq
        c_col = sum_cols[:, h : h + 1]
        c_row = sum_rows[h : h + 1, :]
        beta = gate_cols[:, heads + h : heads + h + 1]
        last = c_col[frames - 1 : frames, :]
        lead = jnp.exp(c_col)
        tail = jnp.exp(last - c_col)
        col_s[h, :, 2:3] = beta
        col_s[h, :, 3:4] = lead
        col_s[h, :, 4:5] = tail
        m = jnp.where(lower, jnp.exp(jnp.where(lower, c_col - c_row, 0.0)), 0.0)
        m_s[h] = m
        both = PREP(jnp.concatenate([kn, qn], axis=0), kn, NT)
        l_mat = jnp.where(strict, beta * m * both[:frames], 0.0)
        l_s[h] = l_mat
        p_s[h] = m * both[frames:]
        strict_parts.append(l_mat)
    inverses = unit_lower_inverse(strict_parts, eye)
    for h in range(heads):
        a = inverses[h]
        a_s[h] = a
        kn = kn_s[h]
        beta = col_s[h, :, 2:3]
        lead = col_s[h, :, 3:4]
        tail = col_s[h, :, 4:5]
        wu = PREP(a, jnp.concatenate([beta * lead * kn, beta * v_all[:, h, :]], axis=1), NN)
        w_s[h] = wu[:, :width]
        u_s[h] = wu[:, width:]
        tk = tail * kn
        ends = PREP(tk, wu, TN)
        map_s[h] = lead[frames - 1 : frames, :] * eye - ends[:, :width]
        shift_s[h] = ends[:, width:]
        inner = PREP(p_s[h], wu, NN)
        qt_s[h] = lead * qn_s[h] - inner[:, :width]
        y0_s[h] = inner[:, width:]
        z_s[h] = PREP(a, tk, TN)

    mask_row = mask_ref[...].astype(F32)
    mask_col = exact(eye, jnp.broadcast_to(mask_row, (8, frames)), NT)[:, 0:1]
    own_s[:, 0:1] = mask_col
    scale = width ** (-0.5)

    def attention():
        for d in range(1, blocks):

            @pl.when(pos >= d)
            def _():
                pltpu.make_async_copy(
                    window.at[d], window.at[d], win_recv_sem.at[d]
                ).wait()

        keys = window[:, 0].reshape(blocks * frames, width)
        values = window[:, 1].reshape(blocks * frames, width)
        t_pos = lax.broadcasted_iota(jnp.int32, (frames, blocks * frames), 0)
        slot = lax.broadcasted_iota(jnp.int32, (frames, blocks * frames), 1)
        distance = slot // frames
        j_pos = slot % frames - distance * frames
        allowed = (j_pos <= t_pos) & (j_pos > t_pos - WIN) & (distance <= pos)
        aq_all = aq_ref[0].astype(F32)
        ro_all = ro_ref[0].astype(F32)
        grad_k = jnp.zeros((blocks * frames, width), F32)
        grad_v = jnp.zeros((blocks * frames, width), F32)
        row_total = jnp.zeros((frames, 1), F32)
        for h in range(heads):
            aq = aq_all[:, h, :].astype(BF16)
            low = (ro_all[:, h, :] * mask_col)
            s = quick(aq, keys, NT) * scale
            s = jnp.where(allowed, s, -jnp.inf)
            e = jnp.exp(s - jnp.max(s, axis=-1, keepdims=True))
            soft = e / jnp.sum(e, axis=-1, keepdims=True)
            weights = soft.astype(BF16)
            out = quick(weights, values, NN)
            row_term = jnp.sum(low * out, axis=-1, keepdims=True)
            row_total = row_total + row_term
            grad_prob = quick(low, values, NT)
            grad_score = (soft * (grad_prob - row_term) * scale).astype(BF16)
            aq_grad_s[h] = quick(grad_score, keys, NN)
            grad_k = grad_k + quick(grad_score, aq, TN)
            grad_v = grad_v + quick(weights, low, TN)
        row_s[...] = jnp.broadcast_to(row_total, row_s.shape)
        own_s[:, width : 2 * width] = grad_k[:frames]
        own_s[:, 2 * width :] = grad_v[:frames]
        for d in range(1, blocks):

            @pl.when(pos >= d)
            def _():
                back_send[d - 1, 0] = grad_k[d * frames : (d + 1) * frames].astype(BF16)
                back_send[d - 1, 1] = grad_v[d * frames : (d + 1) * frames].astype(BF16)
                back_copy(d).start()

    late = pos * 2 >= n
    pl.when(late)(attention)

    for h in range(heads):

        @pl.when(pos == 0)
        def _():
            state_s[h] = s0_ref[0, h]

        @pl.when(pos > 0)
        def _():
            state_copy(h).wait_recv()
            state_s[h] = state_recv[h]

        @pl.when(pos < n - 1)
        def _():
            state_send[h] = shift_s[h] + RELAY(map_s[h], state_s[h], NN)
            state_copy(h).start()

    ro_all = ro_ref[0].astype(F32)
    gdn_rows = jnp.zeros((frames, 1), F32)
    for h in range(heads):
        raw = y0_s[h] + BACK(qt_s[h], state_s[h], NN)
        norm = lax.rsqrt(jnp.mean(raw * raw, axis=-1, keepdims=True) + EPSILON)
        out = raw * norm
        grad = ro_all[:, h, :] * mask_col
        along = jnp.sum(out * grad, axis=-1, keepdims=True)
        gdn_rows = gdn_rows + along
        g_raw = norm * (grad - out * (along * (1.0 / width)))
        g_s[h] = g_raw
        local_s[h] = BACK(qt_s[h], g_raw, TN)

        @pl.when(pos == n - 1)
        def _():
            next_s[h] = jnp.zeros_like(next_s[h])
            grad_send[h] = local_s[h]
            grad_copy(h).start()

    pl.when(jnp.logical_not(late))(attention)

    slot = slot_ref[0]
    sign = 1.0 - 2.0 * (slot % 2).astype(F32)
    tile_pair = lax.broadcasted_iota(jnp.int32, (8, 128), 1)
    member = jnp.where(tile_pair == slot // 2, 1.0, 0.0).astype(F32)
    score = jnp.sum(gdn_rows + row_s[:, 0:1], axis=0, keepdims=True) * total_frames ** (-0.5)
    contribution = member * sign * score
    score_send[...] = contribution
    score_recv[me] = contribution

    def post(j, c):
        score_copy(me, lax.rem(me + j, group)).start()
        return c

    lax.fori_loop(1, group, post, 0)

    for h in range(heads):
        kn = kn_s[h]
        qn = qn_s[h]
        lead = col_s[h, :, 3:4]
        g_raw = g_s[h]
        state = state_s[h]
        delta = u_s[h] - BACK(w_s[h], state, NN)
        delta_s[h] = delta
        b0_s[h] = BACK(a_s[h], BACK(p_s[h], g_raw, TN), TN)
        dp = BACK(g_raw, delta, NT)
        dqk = dp * m_s[h]
        x1 = lead * BACK(g_raw, state, NT)
        dqn = BACK(dqk, kn, NN) + x1
        n_mat = dp * p_s[h]
        local = col_s[h, :, 1:2] * (dqn - qn * jnp.sum(qn * dqn, axis=-1, keepdims=True))
        dq_s[h] = local
        a_s[h] = BACK(dqk, qn, TN)
        p_s[h] = n_mat
        col_s[h, :, 5:6] = jnp.sum(x1 * qn, axis=-1, keepdims=True)

    for h in range(heads):

        @pl.when(pos < n - 1)
        def _():
            grad_copy(h).wait_recv()
            next_s[h] = grad_recv[h]

        @pl.when((pos < n - 1) & (pos > 0))
        def _():
            grad_send[h] = local_s[h] + RELAY(map_s[h], next_s[h], TN)
            grad_copy(h).start()

    def take(j, c):
        score_copy(lax.rem(me + j, group), lax.rem(me + j, group)).wait_recv()
        return c

    lax.fori_loop(1, group, take, 0)
    margin_count = margin_ref.shape[1]
    margin = jnp.sum(score_recv[...], axis=0)[0:1, :margin_count] - margin_ref[...]
    loss = jnp.maximum(-margin, 0.0) + jnp.log1p(jnp.exp(-jnp.abs(margin)))
    loss_ref[...] = jnp.sum(loss, axis=1, keepdims=True)
    pressure = jnp.sum(
        member[0:1, :margin_count] * (1.0 / (1.0 + jnp.exp(margin))), axis=1, keepdims=True
    )
    grad_scale = (total_frames * heads * halves * width) ** 0.5
    coefficient = -grad_scale * sign * pressure * total_frames ** (-0.5)

    dk_list = []
    dv_list = []
    dc_cols = []
    db_cols = []
    n_rows = []
    for h in range(heads):
        kn = kn_s[h]
        rk = col_s[h, :, 0:1]
        beta = col_s[h, :, 2:3]
        lead = col_s[h, :, 3:4]
        tail = col_s[h, :, 4:5]
        later = next_s[h]
        state = state_s[h]
        delta = delta_s[h]
        db = b0_s[h] + BACK(z_s[h], later, NN)
        dl = jnp.where(strict, -BACK(db, delta, NT), 0.0)
        l_term = dl * l_s[h]
        n_mat = p_s[h] + l_term
        dkk = dl * (beta * m_s[h])
        kb = lead * BACK(db, state, NT)
        x2 = -beta * kb
        x3 = tail * BACK(delta, later, NT)
        dkn = a_s[h] + x2 + x3 + BACK(dkk, kn, NN) + BACK(dkk, kn, TN)
        v_h = v_ref[0].astype(F32)[:, h, :]
        dk_list.append(rk * (dkn - kn * jnp.sum(kn * dkn, axis=-1, keepdims=True)))
        dv_list.append(beta * db)
        db_cols.append(
            jnp.sum(db * v_h - kb * kn, axis=-1, keepdims=True)
            + jnp.sum(l_term, axis=-1, keepdims=True) / beta
        )
        tail_term = jnp.sum(x3 * kn, axis=-1, keepdims=True)
        end_term = jnp.sum(tail_term, axis=0, keepdims=True) + lead[
            frames - 1 : frames, :
        ] * jnp.sum(jnp.sum(later * state, axis=-1, keepdims=True), axis=0, keepdims=True)
        dc = (
            jnp.sum(n_mat, axis=-1, keepdims=True)
            + col_s[h, :, 5:6]
            + jnp.sum(x2 * kn, axis=-1, keepdims=True)
            - tail_term
        )
        dc = dc + jnp.where(rows[:, 0:1] == frames - 1, end_term, 0.0)
        dc_cols.append(dc)
        n_rows.append(jnp.sum(n_mat, axis=0, keepdims=True))
    cols_all = jnp.concatenate(dc_cols + db_cols, axis=1)
    pad = [jnp.zeros((heads, frames), F32)]
    n_all = jnp.concatenate(n_rows + pad, axis=0)
    dg = (exact(cols_all, tri, TN) - exact(n_all, tri, NN))[:heads]
    dbeta = exact(cols_all, eye, TN)[heads:]
    dg_ref[0] = coefficient * dg
    db_ref[0] = coefficient * dbeta
    dq_ref[0] = jnp.stack([dq_s[h] * coefficient for h in range(heads)], axis=1).astype(BF16)
    dk_ref[0] = jnp.stack([x * coefficient for x in dk_list], axis=1).astype(BF16)
    dv_ref[0] = jnp.stack([x * coefficient for x in dv_list], axis=1).astype(BF16)
    daq_ref[0] = jnp.stack(
        [aq_grad_s[h] * coefficient for h in range(heads)], axis=1
    ).astype(BF16)

    for d in range(1, blocks):

        @pl.when(pos + d < n)
        def _():
            pltpu.make_async_copy(
                back_recv.at[d - 1], back_recv.at[d - 1], back_recv_sem.at[d]
            ).wait()
            own_s[:, width : 2 * width] += back_recv[d - 1, 0].astype(F32)
            own_s[:, 2 * width :] += back_recv[d - 1, 1].astype(F32)

    dak_ref[0] = (own_s[:, width : 2 * width] * coefficient).astype(BF16)[:, None, :]
    dav_ref[0] = (own_s[:, 2 * width :] * coefficient).astype(BF16)[:, None, :]

    for d in range(1, blocks):

        @pl.when(pos + d < n)
        def _():
            window_copy(d).wait_send()

        @pl.when(pos >= d)
        def _():
            back_copy(d).wait_send()

    for h in range(heads):

        @pl.when(pos < n - 1)
        def _():
            state_copy(h).wait_send()

        @pl.when(pos > 0)
        def _():
            grad_copy(h).wait_send()

    def sent(j, c):
        score_copy(me, lax.rem(me + j, group)).wait_send()
        return c

    lax.fori_loop(1, group, sent, 0)


def body(
    sizes,
    gdn_query,
    gdn_key,
    gdn_value,
    log_decay,
    write_rate,
    init_state,
    attn_query,
    attn_key,
    attn_value,
    readout,
    speaker_mask,
    pair_slot,
    ref_margin,
):
    n, pairs, halves = sizes
    group = n * pairs * halves
    seq, frames, heads, width = gdn_query.shape
    blocks = min(WIN // frames, n - 1) + 1
    vmem = pl.BlockSpec(memory_space=pltpu.VMEM)
    smem = pl.BlockSpec(memory_space=pltpu.SMEM)
    dma = pltpu.SemaphoreType.DMA
    square = pltpu.VMEM((heads, frames, width), F32)
    state_square = pltpu.VMEM((heads, width, width), F32)
    shape = jax.ShapeDtypeStruct
    out = pl.pallas_call(
        functools.partial(kernel, sizes),
        out_shape=(
            shape((1, 1), F32),
            shape(gdn_query.shape, BF16),
            shape(gdn_key.shape, BF16),
            shape(gdn_value.shape, BF16),
            shape(log_decay.shape, F32),
            shape(write_rate.shape, F32),
            shape(attn_query.shape, BF16),
            shape(attn_key.shape, BF16),
            shape(attn_value.shape, BF16),
        ),
        in_specs=[vmem] * 11 + [smem, vmem],
        out_specs=(vmem,) * 9,
        scratch_shapes=[
            pltpu.VMEM((blocks, 2, frames, width), BF16),
            pltpu.VMEM((blocks - 1, 2, frames, width), BF16),
            pltpu.VMEM((blocks - 1, 2, frames, width), BF16),
            state_square,
            state_square,
            state_square,
            state_square,
            pltpu.VMEM((8, 128), F32),
            pltpu.VMEM((group, 8, 128), F32),
        ]
        + [square] * 13
        + [pltpu.VMEM((heads, frames, 128), F32)]
        + [square] * 8
        + [pltpu.VMEM((frames, 3 * width), F32), pltpu.VMEM((frames, 128), F32)]
        + [
            dma((blocks,)),
            dma((blocks,)),
            dma((blocks,)),
            dma((blocks,)),
            dma((heads,)),
            dma((heads,)),
            dma((heads,)),
            dma((heads,)),
            dma((group,)),
            dma((group,)),
        ],
        compiler_params=pltpu.CompilerParams(
            collective_id=0, has_side_effects=True, vmem_limit_bytes=40 * 1024 * 1024
        ),
    )(
        gdn_query,
        gdn_key,
        gdn_value,
        log_decay,
        write_rate,
        init_state,
        attn_query,
        attn_key,
        attn_value,
        readout,
        speaker_mask,
        pair_slot,
        ref_margin.reshape(1, -1),
    )
    return (out[0].reshape(1),) + tuple(out[1:])


def solution(mesh):
    sizes = (mesh.shape["tm"], mesh.shape["pair"], mesh.shape["head"])
    wide = P(("groups", "pair"), "tm", "head", None)
    gate = P(("groups", "pair"), "head", "tm")
    return jax.shard_map(
        functools.partial(body, sizes),
        mesh=mesh,
        in_specs=(
            wide,
            wide,
            wide,
            gate,
            gate,
            P(("groups", "pair"), "head", None, None),
            wide,
            wide,
            wide,
            wide,
            P(("groups", "pair"), "tm"),
            P(("groups", "pair")),
            P("groups"),
        ),
        out_specs=(P("groups"), wide, wide, wide, gate, gate, wide, wide, wide),
        check_vma=False,
    )
```

profile of v0, /device:TPU:0, one launch (start us, length us, event | category | flops | bytes accessed | tf_op | source)
XLA Modules:
  0.0 65.0 jit_solution(7379768770551640365)
XLA Ops:
  0.6 0.0 copy-start.1
  2.0 0.8 %copy.22.ak_ref = bf16[1,128,1,128]{3,2,1,0:T(2,128)(2,1)S(1)} copy(bf16[1,128,1,128]{3,1,2,0:T(8,128)(2,1)} %param.20) | data formatting | bytes 65536 | tf_op args[7]
  2.8 0.0 copy-start.6
  2.8 0.0 copy-start.7
  2.8 0.0 copy-start.8
  2.8 0.8 %copy.23.av_ref = bf16[1,128,1,128]{3,2,1,0:T(2,128)(2,1)S(1)} copy(bf16[1,128,1,128]{3,1,2,0:T(8,128)(2,1)} %param.21) | data formatting | bytes 65536 | tf_op args[8]
  3.7 0.0 copy-done.1
  3.7 0.0 copy-done.6
  3.7 0.0 copy-done.7
  3.7 0.0 copy-done.8
  3.7 0.0 copy-start
  3.7 0.9 %copy-done = f32[1,4,128,128]{3,2,1,0:T(8,128)S(1)} copy-done((f32[1,4,128,128]{3,2,1,0:T(8,128)S(1)}, f32[1,4,128,128]{3,2,1,0:T(8,128)}, u32[]{:S(2)}) %copy-start) | copy-done | bytes 262168
  4.6 0.0 copy-start.2
  4.6 0.9 %copy-done.2 = bf16[1,128,4,128]{3,2,1,0:T(4,128)(2,1)S(1)} copy-done((bf16[1,128,4,128]{3,2,1,0:T(4,128)(2,1)S(1)}, bf16[1,128,4,128]{3,2,1,0:T(4,128)(2,1)}, u32[]{:S(2)}) %copy-start.2) | copy-done | bytes 131096
  5.6 0.0 copy-start.3
  5.6 0.9 %copy-done.3 = bf16[1,128,4,128]{3,2,1,0:T(4,128)(2,1)S(1)} copy-done((bf16[1,128,4,128]{3,2,1,0:T(4,128)(2,1)S(1)}, bf16[1,128,4,128]{3,2,1,0:T(4,128)(2,1)}, u32[]{:S(2)}) %copy-start.3) | copy-done | bytes 131096
  6.5 0.0 copy-start.4
  6.5 0.9 %copy-done.4 = bf16[1,128,4,128]{3,2,1,0:T(4,128)(2,1)S(1)} copy-done((bf16[1,128,4,128]{3,2,1,0:T(4,128)(2,1)S(1)}, bf16[1,128,4,128]{3,2,1,0:T(4,128)(2,1)}, u32[]{:S(2)}) %copy-start.4) | copy-done | bytes 131096
  7.4 0.0 copy-start.5
  7.4 0.9 %copy-done.5 = bf16[1,128,4,128]{3,2,1,0:T(4,128)(2,1)S(1)} copy-done((bf16[1,128,4,128]{3,2,1,0:T(4,128)(2,1)S(1)}, bf16[1,128,4,128]{3,2,1,0:T(4,128)(2,1)}, u32[]{:S(2)}) %copy-start.5) | copy-done | bytes 131096
  8.3 49.9 %shard_map.196 = (f32[1,1]{1,0:T(1,128)}, bf16[1,128,4,128]{3,2,1,0:T(4,128)(2,1)S(1)}, bf16[1,128,4,128]{3,2,1,0:T(4,128)(2,1)S(1)}, bf16[1,128,4,128]{3,2,1,0:...) custom-call(bf16[1,128,4,128]{3,2,1,0:T(4,128)(2,1)S(1)} %copy-done., ...), custom_call_target="tpu_custom_call" | custom-call | tf_op jit(solution)/shard_map/pallas_call | solution.py:559
  58.2 0.6 copy.24
  58.8 0.6 copy.25
  60.1 0.7 %copy.36 = bf16[1,128,4,128]{3,2,1,0:T(4,128)(2,1)} copy(bf16[1,128,4,128]{3,2,1,0:T(4,128)(2,1)S(1)} %get-tuple-element.46) | data formatting | bytes 262144
  60.8 0.7 %copy.37 = bf16[1,128,4,128]{3,2,1,0:T(4,128)(2,1)} copy(bf16[1,128,4,128]{3,2,1,0:T(4,128)(2,1)S(1)} %get-tuple-element.47) | data formatting | bytes 262144
  61.4 0.7 %copy.38 = bf16[1,128,4,128]{3,2,1,0:T(4,128)(2,1)} copy(bf16[1,128,4,128]{3,2,1,0:T(4,128)(2,1)S(1)} %get-tuple-element.48) | data formatting | bytes 262144
  62.1 0.6 copy.39
  62.6 0.6 copy.40
  63.2 0.7 %copy.41 = bf16[1,128,4,128]{3,2,1,0:T(4,128)(2,1)} copy(bf16[1,128,4,128]{3,2,1,0:T(4,128)(2,1)S(1)} %get-tuple-element.51) | data formatting | bytes 262144
Async XLA Ops:
  0.6 3.0 %copy-start.1 = (bf16[1,128,4,128]{3,2,1,0:T(4,128)(2,1)S(1)}, bf16[1,128,4,128]{3,2,1,0:T(4,128)(2,1)}, u32[]{:S(2)}) copy-start(bf16[1,128,4,128]{3,2,1,0:T(4,128)(2,1)} %q_ref.1) | copy-start | bytes 393220
  2.8 0.9 %copy-start.6 = (f32[1,4,128]{2,1,0:T(4,128)S(1)}, f32[1,4,128]{2,1,0:T(4,128)}, u32[]{:S(2)}) copy-start(f32[1,4,128]{2,1,0:T(4,128)} %g_ref.1) | copy-start | bytes 6148
  2.8 0.9 %copy-start.7 = (f32[1,4,128]{2,1,0:T(4,128)S(1)}, f32[1,4,128]{2,1,0:T(4,128)}, u32[]{:S(2)}) copy-start(f32[1,4,128]{2,1,0:T(4,128)} %b_ref.1) | copy-start | bytes 6148
  2.8 0.9 %copy-start.8 = (s32[1,128]{1,0:T(1,128)S(1)}, s32[1,128]{1,0:T(1,128)}, u32[]{:S(2)}) copy-start(s32[1,128]{1,0:T(1,128)} %mask_ref.1) | copy-start | bytes 1540
  3.7 1.0 %copy-start = (f32[1,4,128,128]{3,2,1,0:T(8,128)S(1)}, f32[1,4,128,128]{3,2,1,0:T(8,128)}, u32[]{:S(2)}) copy-start(f32[1,4,128,128]{3,2,1,0:T(8,128)} %s0_ref.1) | copy-start | bytes 786436
  4.6 0.9 %copy-start.2 = (bf16[1,128,4,128]{3,2,1,0:T(4,128)(2,1)S(1)}, bf16[1,128,4,128]{3,2,1,0:T(4,128)(2,1)}, u32[]{:S(2)}) copy-start(bf16[1,128,4,128]{3,2,1,0:T(4,128)(2,1)} %k_ref.1) | copy-start | bytes 393220
  5.6 0.9 %copy-start.3 = (bf16[1,128,4,128]{3,2,1,0:T(4,128)(2,1)S(1)}, bf16[1,128,4,128]{3,2,1,0:T(4,128)(2,1)}, u32[]{:S(2)}) copy-start(bf16[1,128,4,128]{3,2,1,0:T(4,128)(2,1)} %v_ref.1) | copy-start | bytes 393220
  6.5 0.9 %copy-start.4 = (bf16[1,128,4,128]{3,2,1,0:T(4,128)(2,1)S(1)}, bf16[1,128,4,128]{3,2,1,0:T(4,128)(2,1)}, u32[]{:S(2)}) copy-start(bf16[1,128,4,128]{3,2,1,0:T(4,128)(2,1)} %aq_ref.1) | copy-start | bytes 393220
  7.4 0.9 %copy-start.5 = (bf16[1,128,4,128]{3,2,1,0:T(4,128)(2,1)S(1)}, bf16[1,128,4,128]{3,2,1,0:T(4,128)(2,1)}, u32[]{:S(2)}) copy-start(bf16[1,128,4,128]{3,2,1,0:T(4,128)(2,1)} %ro_ref.1) | copy-start | bytes 393220
where the time goes:
time: 65.4 us; the launch traced here: 65 us
  Pallas kernels  49.9 us (76%)
  local copies, waits for them, and re-layouts  11.2 us (17%)
  between operations  3.82 us (6%)
    pallas_call x1, Pallas kernels, body(): pl.pallas_call(functools.partial(kernel, sizes), out_shape=(shape((1, 1),...  49.9 us
    unnamed x28, local copies, waits for them, and re-layouts  11.2 us

commit v1 on v0

--- a/solution.py
+++ b/solution.py
@@ -40,10 +40,10 @@
     return dot(a_high, b_high) + (dot(a_high, b_low) + dot(a_low, b_high))
 
 
-INVERT = exact
-PREP = exact
-RELAY = exact
-BACK = exact
+INVERT = triple
+PREP = triple
+RELAY = triple
+BACK = triple
 
 
 def unit_lower_inverse(strict, eye):
@@ -59,6 +59,7 @@
 
 def kernel(
     sizes,
+    fetches,
     q_ref,
     k_ref,
     v_ref,
@@ -66,8 +67,6 @@
     b_ref,
     s0_ref,
     aq_ref,
-    ak_ref,
-    av_ref,
     ro_ref,
     mask_ref,
     slot_ref,
@@ -203,8 +202,8 @@
             device_id_type=pl.DeviceIdType.MESH,
         )
 
-    window[0, 0] = ak_ref[0, :, 0, :]
-    window[0, 1] = av_ref[0, :, 0, :]
+    fetches[7].wait()
+    fetches[8].wait()
     pl.semaphore_wait(barrier, group - 1)
     for d in range(1, blocks):
 
@@ -223,6 +222,8 @@
     tri = jnp.where(lower, 1.0, 0.0).astype(F32)
     eye = jnp.where(rows == cols, 1.0, 0.0).astype(F32)
 
+    for i in (3, 4, 1, 0, 2, 10, 5, 6, 9):
+        fetches[i].wait()
     gates = jnp.concatenate([g_ref[0], b_ref[0]], axis=0)
     sum_rows = exact(gates, tri, NT)
     sum_cols = exact(tri, gates, NT)
@@ -398,11 +399,11 @@
         dp = BACK(g_raw, delta, NT)
         dqk = dp * m_s[h]
         x1 = lead * BACK(g_raw, state, NT)
-        dqn = BACK(dqk, kn, NN) + x1
+        dqn = quick(dqk, kn, NN) + x1
         n_mat = dp * p_s[h]
         local = col_s[h, :, 1:2] * (dqn - qn * jnp.sum(qn * dqn, axis=-1, keepdims=True))
         dq_s[h] = local
-        a_s[h] = BACK(dqk, qn, TN)
+        a_s[h] = quick(dqk, qn, TN)
         p_s[h] = n_mat
         col_s[h, :, 5:6] = jnp.sum(x1 * qn, axis=-1, keepdims=True)
 
@@ -455,7 +456,7 @@
         kb = lead * BACK(db, state, NT)
         x2 = -beta * kb
         x3 = tail * BACK(delta, later, NT)
-        dkn = a_s[h] + x2 + x3 + BACK(dkk, kn, NN) + BACK(dkk, kn, TN)
+        dkn = a_s[h] + x2 + x3 + quick(dkk, kn, NN) + quick(dkk, kn, TN)
         v_h = v_ref[0].astype(F32)[:, h, :]
         dk_list.append(rk * (dkn - kn * jnp.sum(kn * dkn, axis=-1, keepdims=True)))
         dv_list.append(beta * db)
@@ -500,8 +501,8 @@
             own_s[:, width : 2 * width] += back_recv[d - 1, 0].astype(F32)
             own_s[:, 2 * width :] += back_recv[d - 1, 1].astype(F32)
 
-    dak_ref[0] = (own_s[:, width : 2 * width] * coefficient).astype(BF16)[:, None, :]
-    dav_ref[0] = (own_s[:, 2 * width :] * coefficient).astype(BF16)[:, None, :]
+    dak_ref[...] = (own_s[:, width : 2 * width] * coefficient).astype(BF16)
+    dav_ref[...] = (own_s[:, 2 * width :] * coefficient).astype(BF16)
 
     for d in range(1, blocks):
 
@@ -528,6 +529,35 @@
         return c
 
     lax.fori_loop(1, group, sent, 0)
+
+
+def entry(sizes, *refs):
+    sources, small = refs[:11], refs[11:13]
+    results, rest = refs[13:22], refs[22:]
+    held, fetch_sem, scratch = rest[:9], rest[9], rest[10:]
+    window = scratch[0]
+    targets = list(held[:7]) + [window.at[0, 0], window.at[0, 1]] + list(held[7:])
+    copies = [
+        pltpu.make_async_copy(source, target, fetch_sem.at[i])
+        for i, (source, target) in enumerate(zip(sources, targets))
+    ]
+    for i in FETCH_ORDER:
+        copies[i].start()
+    kernel(sizes, copies, *held, *small, *results, *scratch)
+
+
+def hand_over(*refs):
+    count = (len(refs) - 1) // 2
+    copies = [
+        pltpu.make_async_copy(refs[i], refs[count + i], refs[-1].at[i]) for i in range(count)
+    ]
+    for copy in copies:
+        copy.start()
+    for copy in copies:
+        copy.wait()
+
+
+FETCH_ORDER = (7, 8, 3, 4, 1, 0, 2, 10, 5, 6, 9)
 
 
 def body(
@@ -551,13 +581,14 @@
     seq, frames, heads, width = gdn_query.shape
     blocks = min(WIN // frames, n - 1) + 1
     vmem = pl.BlockSpec(memory_space=pltpu.VMEM)
+    hbm = pl.BlockSpec(memory_space=pltpu.HBM)
     smem = pl.BlockSpec(memory_space=pltpu.SMEM)
     dma = pltpu.SemaphoreType.DMA
     square = pltpu.VMEM((heads, frames, width), F32)
     state_square = pltpu.VMEM((heads, width, width), F32)
     shape = jax.ShapeDtypeStruct
     out = pl.pallas_call(
-        functools.partial(kernel, sizes),
+        functools.partial(entry, sizes),
         out_shape=(
             shape((1, 1), F32),
             shape(gdn_query.shape, BF16),
@@ -566,12 +597,19 @@
             shape(log_decay.shape, F32),
             shape(write_rate.shape, F32),
             shape(attn_query.shape, BF16),
-            shape(attn_key.shape, BF16),
-            shape(attn_value.shape, BF16),
+            shape((frames, width), BF16),
+            shape((frames, width), BF16),
         ),
-        in_specs=[vmem] * 11 + [smem, vmem],
+        in_specs=[hbm] * 11 + [smem, vmem],
         out_specs=(vmem,) * 9,
-        scratch_shapes=[
+        scratch_shapes=[pltpu.VMEM(gdn_query.shape, BF16)] * 3
+        + [pltpu.VMEM(log_decay.shape, F32)] * 2
+        + [
+            pltpu.VMEM(init_state.shape, F32),
+            pltpu.VMEM(attn_query.shape, BF16),
+            pltpu.VMEM(readout.shape, BF16),
+            pltpu.VMEM(speaker_mask.shape, jnp.int32),
+            dma((11,)),
             pltpu.VMEM((blocks, 2, frames, width), BF16),
             pltpu.VMEM((blocks - 1, 2, frames, width), BF16),
             pltpu.VMEM((blocks - 1, 2, frames, width), BF16),
@@ -599,7 +637,7 @@
             dma((group,)),
         ],
         compiler_params=pltpu.CompilerParams(
-            collective_id=0, has_side_effects=True, vmem_limit_bytes=40 * 1024 * 1024
+            collective_id=0, has_side_effects=True, vmem_limit_bytes=62 * 1024 * 1024
         ),
     )(
         gdn_query,
@@ -609,14 +647,26 @@
         write_rate,
         init_state,
         attn_query,
-        attn_key,
-        attn_value,
+        attn_key.reshape(frames, width),
+        attn_value.reshape(frames, width),
         readout,
         speaker_mask,
         pair_slot,
         ref_margin.reshape(1, -1),
     )
-    return (out[0].reshape(1),) + tuple(out[1:])
+    final = pl.pallas_call(
+        hand_over,
+        out_shape=tuple(shape(a.shape, a.dtype) for a in out[1:]),
+        in_specs=[hbm] * 8,
+        out_specs=(hbm,) * 8,
+        scratch_shapes=[dma((8,))],
+        compiler_params=pltpu.CompilerParams(vmem_limit_bytes=62 * 1024 * 1024),
+    )(*out[1:])
+    return (
+        (out[0].reshape(1),)
+        + tuple(final[:6])
+        + (final[6].reshape(attn_key.shape), final[7].reshape(attn_value.shape))
+    )
 
 
 def solution(mesh):

time: 65.4 us -> 70.1 us (1.072)
  Pallas kernels: 49.9 us -> 66.2 us
  local copies, waits for them, and re-layouts: 11.2 us -> 0 us
    pallas_call x1 -> x2, Pallas kernels: 49.9 us -> 66.2 us  [the longest x1 47.1 us: body(): pl.pallas_call(functools.partial(entry, sizes), out_shape=(shape((1, 1),...]
    unnamed x28 -> x0, local copies, waits for them, and re-layouts: 11.2 us -> none
where the time goes in v1:
time: 70.1 us; the launch traced here: 69.9 us
  Pallas kernels  66.2 us (94%)
  between operations  3.7 us (5%)
    pallas_call x1, Pallas kernels, body(): pl.pallas_call(functools.partial(entry, sizes), out_shape=(shape((1, 1),...  47.1 us
    pallas_call x1, Pallas kernels, body(): pl.pallas_call(hand_over, out_shape=tuple((shape(a.shape, a.dtype) for a...  19.2 us

profile of v1, /device:TPU:0, one launch (start us, length us, event | category | flops | bytes accessed | tf_op | source)
XLA Modules:
  0.0 69.9 jit_solution(14829584861484378806)
XLA Ops:
  1.9 47.1 %shard_map.196 = (f32[1,1]{1,0:T(1,128)}, bf16[1,128,4,128]{3,2,1,0:T(4,128)(2,1)}, bf16[1,128,4,128]{3,2,1,0:T(4,128)(2,1)}, bf16[1,128,4,128]{3,2,1,0:T(4,128)...) custom-call(bf16[1,128,4,128]{3,2,1,0:T(4,128)(2,1)} %refs_0_.1, ...), custom_call_target="tpu_custom_call" | custom-call | tf_op jit(solution)/shard_map/pallas_call | solution.py:590
  49.0 19.2 %shard_map.197 = (bf16[1,128,4,128]{3,2,1,0:T(4,128)(2,1)}, bf16[1,128,4,128]{3,2,1,0:T(4,128)(2,1)}, bf16[1,128,4,128]{3,2,1,0:T(4,128)(2,1)}, f32[1,4,128]{2,1...) custom-call(bf16[1,128,4,128]{3,2,1,0:T(4,128)(2,1)} %get-tuple-elem, ...), custom_call_target="tpu_custom_call" | custom-call | tf_op jit(solution)/shard_map/pallas_call | solution.py:657

commit v2 on v1

--- a/solution.py
+++ b/solution.py
@@ -92,6 +92,7 @@
     kn_s,
     qn_s,
     map_s,
+    map_t_s,
     shift_s,
     qt_s,
     y0_s,
@@ -222,7 +223,7 @@
     tri = jnp.where(lower, 1.0, 0.0).astype(F32)
     eye = jnp.where(rows == cols, 1.0, 0.0).astype(F32)
 
-    for i in (3, 4, 1, 0, 2, 10, 5, 6, 9):
+    for i in (3, 4, 1, 0, 2):
         fetches[i].wait()
     gates = jnp.concatenate([g_ref[0], b_ref[0]], axis=0)
     sum_rows = exact(gates, tri, NT)
@@ -272,13 +273,17 @@
         u_s[h] = wu[:, width:]
         tk = tail * kn
         ends = PREP(tk, wu, TN)
-        map_s[h] = lead[frames - 1 : frames, :] * eye - ends[:, :width]
+        state_map = lead[frames - 1 : frames, :] * eye - ends[:, :width]
+        map_s[h] = state_map
+        map_t_s[h] = state_map.T
         shift_s[h] = ends[:, width:]
         inner = PREP(p_s[h], wu, NN)
         qt_s[h] = lead * qn_s[h] - inner[:, :width]
         y0_s[h] = inner[:, width:]
         z_s[h] = PREP(a, tk, TN)
 
+    for i in (10, 5, 6, 9):
+        fetches[i].wait()
     mask_row = mask_ref[...].astype(F32)
     mask_col = exact(eye, jnp.broadcast_to(mask_row, (8, frames)), NT)[:, 0:1]
     own_s[:, 0:1] = mask_col
@@ -388,6 +393,15 @@
     lax.fori_loop(1, group, post, 0)
 
     for h in range(heads):
+
+        @pl.when((pos < n - 1) & (pos > 0))
+        def _():
+            grad_copy(h).wait_recv()
+            next_s[h] = grad_recv[h]
+            grad_send[h] = local_s[h] + RELAY(map_t_s[h], next_s[h], NN)
+            grad_copy(h).start()
+
+    for h in range(heads):
         kn = kn_s[h]
         qn = qn_s[h]
         lead = col_s[h, :, 3:4]
@@ -409,15 +423,10 @@
 
     for h in range(heads):
 
-        @pl.when(pos < n - 1)
+        @pl.when(pos == 0)
         def _():
             grad_copy(h).wait_recv()
             next_s[h] = grad_recv[h]
-
-        @pl.when((pos < n - 1) & (pos > 0))
-        def _():
-            grad_send[h] = local_s[h] + RELAY(map_s[h], next_s[h], TN)
-            grad_copy(h).start()
 
     def take(j, c):
         score_copy(lax.rem(me + j, group), lax.rem(me + j, group)).wait_recv()
@@ -547,13 +556,17 @@
 
 
 def hand_over(*refs):
-    count = (len(refs) - 1) // 2
-    copies = [
-        pltpu.make_async_copy(refs[i], refs[count + i], refs[-1].at[i]) for i in range(count)
-    ]
-    for copy in copies:
+    count = (len(refs) - 2) // 3
+    into, away = refs[-2:]
+    held = refs[2 * count : 3 * count]
+    taken = [pltpu.make_async_copy(refs[i], held[i], into.at[i]) for i in range(count)]
+    given = [pltpu.make_async_copy(held[i], refs[count + i], away.at[i]) for i in range(count)]
+    for copy in taken:
         copy.start()
-    for copy in copies:
+    for first, second in zip(taken, given):
+        first.wait()
+        second.start()
+    for copy in given:
         copy.wait()
 
 
@@ -620,7 +633,7 @@
             pltpu.VMEM((8, 128), F32),
             pltpu.VMEM((group, 8, 128), F32),
         ]
-        + [square] * 13
+        + [square] * 14
         + [pltpu.VMEM((heads, frames, 128), F32)]
         + [square] * 8
         + [pltpu.VMEM((frames, 3 * width), F32), pltpu.VMEM((frames, 128), F32)]
@@ -659,7 +672,7 @@
         out_shape=tuple(shape(a.shape, a.dtype) for a in out[1:]),
         in_specs=[hbm] * 8,
         out_specs=(hbm,) * 8,
-        scratch_shapes=[dma((8,))],
+        scratch_shapes=[pltpu.VMEM(a.shape, a.dtype) for a in out[1:]] + [dma((8,)), dma((8,))],
         compiler_params=pltpu.CompilerParams(vmem_limit_bytes=62 * 1024 * 1024),
     )(*out[1:])
     return (

time: 70.1 us -> 52.6 us (0.75)
  Pallas kernels: 66.2 us -> 48.7 us
    pallas_call x1, Pallas kernels: 19.2 us -> 1.91 us  [body(): pl.pallas_call(hand_over, out_shape=tuple((shape(a.shape, a.dtype) for a...]
where the time goes in v2:
time: 52.6 us; the launch traced here: 52.4 us
  Pallas kernels  48.7 us (93%)
  between operations  3.7 us (7%)
    pallas_call x1, Pallas kernels, body(): pl.pallas_call(functools.partial(entry, sizes), out_shape=(shape((1, 1),...  46.8 us
    pallas_call x1, Pallas kernels, body(): pl.pallas_call(hand_over, out_shape=tuple((shape(a.shape, a.dtype) for a...  1.91 us

profile of v2, /device:TPU:0, one launch (start us, length us, event | category | flops | bytes accessed | tf_op | source)
XLA Modules:
  0.0 52.4 jit_solution(1471621019680283173)
XLA Ops:
  1.9 46.8 %shard_map.196 = (f32[1,1]{1,0:T(1,128)}, bf16[1,128,4,128]{3,2,1,0:T(4,128)(2,1)}, bf16[1,128,4,128]{3,2,1,0:T(4,128)(2,1)}, bf16[1,128,4,128]{3,2,1,0:T(4,128)...) custom-call(bf16[1,128,4,128]{3,2,1,0:T(4,128)(2,1)} %refs_0_.1, ...), custom_call_target="tpu_custom_call" | custom-call | tf_op jit(solution)/shard_map/pallas_call | solution.py:603
  48.7 1.9 %shard_map.197 = (bf16[1,128,4,128]{3,2,1,0:T(4,128)(2,1)}, bf16[1,128,4,128]{3,2,1,0:T(4,128)(2,1)}, bf16[1,128,4,128]{3,2,1,0:T(4,128)(2,1)}, f32[1,4,128]{2,1...) custom-call(bf16[1,128,4,128]{3,2,1,0:T(4,128)(2,1)} %get-tuple-elem, ...), custom_call_target="tpu_custom_call" | custom-call | tf_op jit(solution)/shard_map/pallas_call | solution.py:670
